TPU v7x, 512 devices: a whole 4x4x16 slice. The times are simulated.
512 devices in a mesh: patch: 64 (over x, z_lo, core), head: 8 (over y, z_hi).
Axes of the slice: x: 4, y: 4, z: 16 (z_hi: 2, z_lo: 8; z = z_hi * 8 + z_lo), core: 2. Of those that a mesh axis runs over, the one named last changes fastest.
Arguments:
- queries: bfloat16 [3072, 3072], P('patch', 'head'), as said below
- stale_kv: bfloat16 [2, 3072, 3072], P(None, None, 'head'), may hold values from -6 to 6, as said below
- codes: int32 [2, 3072, 3072], P(None, 'patch', 'head'), may hold values from -127 to 127
- exponents: int32 [2, 3072, 24], P(None, 'patch', 'head'), may hold values from -9 to -6
- text_kv: bfloat16 [2, 512, 3072], P(None, None, 'head'), may hold values from -6 to 6, as said below
- out_weight: bfloat16 [3072, 3072], P('head', 'patch'), may hold values from -0.109375 to 0.109375
- out_bias: float32 [3072], P('head'), may hold values from -0.6 to 0.6
- out_gate: float32 [3072], P('head'), may hold values from 2 to 8
Outputs:
- gated_out: bfloat16 [3072, 3072], P('patch', 'head')
Inputs may be any that keep to these rules, and one draw needn't show every extreme that they name: queries are real-valued. `stale_kv`: last step's keys and values are real-valued. `text_kv`: text keys and values are real-valued.
All inputs are finite; a program needn't handle non-finite values.
Results may differ from a plain program's by a relative error of at most 0.0075.
Values may be sent and summed in bfloat16 or wider, within the bound.
A program may use at most 64 MiB of HBM per device.

v0:
```python
import jax
import jax.numpy as jnp
from jax import lax
from jax.sharding import PartitionSpec as P

HD = 128


def body(queries, stale_kv, codes, exponents, text_kv, out_weight, out_bias, out_gate):
    tok_rows = queries.shape[0]
    row_width = queries.shape[1]
    head_count = row_width // HD
    text_count = text_kv.shape[1]
    scale_factor = HD ** (-0.5)
    blocks = jnp.exp2(exponents.astype(jnp.float32))
    decoded = codes.astype(jnp.float32).reshape(2, tok_rows, head_count, HD) * blocks[..., None]
    decoded = decoded.astype(jnp.bfloat16).reshape(2, tok_rows, row_width)
    arrived = lax.all_gather(decoded, "patch", axis=1, tiled=True)
    all_rows = arrived.shape[1]
    query_heads = queries.reshape(tok_rows, head_count, HD)
    text_heads = text_kv.reshape(2, text_count, head_count, HD)
    stale_heads = stale_kv.reshape(2, all_rows, head_count, HD)
    arrived_heads = arrived.reshape(2, all_rows, head_count, HD)
    text_scores = jnp.einsum(
        "thd,khd->htk", query_heads, text_heads[0], preferred_element_type=jnp.float32
    )
    rebuilt = stale_heads.astype(jnp.float32) + arrived_heads.astype(jnp.float32)
    image_scores = jnp.einsum(
        "thd,khd->htk", query_heads.astype(jnp.float32), rebuilt[0], precision=lax.Precision.HIGHEST
    )
    scores = jnp.concatenate([text_scores, image_scores], axis=2) * scale_factor
    row_peak = jnp.max(scores, axis=2, keepdims=True)
    weights = jnp.exp(scores - row_peak).astype(jnp.bfloat16)
    row_total = jnp.sum(weights.astype(jnp.float32), axis=2)
    text_part = jnp.einsum(
        "htk,khd->thd",
        weights[:, :, :text_count],
        text_heads[1],
        preferred_element_type=jnp.float32,
    )
    image_weights = weights[:, :, text_count:]
    image_part = jnp.einsum(
        "htk,khd->thd",
        image_weights.astype(jnp.float32),
        rebuilt[1],
        precision=lax.Precision.HIGHEST,
    )
    attended = (
        ((text_part + image_part) / row_total.T[:, :, None])
        .astype(jnp.bfloat16)
        .reshape(tok_rows, row_width)
    )
    partial_terms = jnp.dot(
        attended,
        lax.all_gather(out_weight, "patch", axis=1, tiled=True),
        preferred_element_type=jnp.float32,
    )
    column_share = lax.psum_scatter(partial_terms, "head", scatter_dimension=1, tiled=True)
    return (out_gate * (column_share + out_bias)).astype(jnp.bfloat16)


def solution(mesh):
    placed = (
        P("patch", "head"),
        P(None, None, "head"),
        P(None, "patch", "head"),
        P(None, "patch", "head"),
        P(None, None, "head"),
        P("head", "patch"),
        P("head"),
        P("head"),
    )
    return jax.shard_map(
        body, mesh=mesh, in_specs=placed, out_specs=P("patch", "head"), check_vma=False
    )
```

profile of v0, /device:TPU:6, one launch (start us, length us, event | category | flops | bytes accessed | tf_op | source)
XLA Modules:
  0.0 375.7 jit_solution(16751030778900406837)
XLA Ops:
  6.5 0.7 multiply_exponential_fusion
  7.2 0.1 copy.15
  7.3 0.2 mul.26
  7.5 0.1 mul.27
  7.6 1.6 multiply_convert_fusion
  9.2 0.0 all-gather.5.cloned.1.call-start
  9.3 0.7 all-gather.5.cloned.1.call-update
  10.0 1.2 fusion.23
  11.2 0.2 copy.28
  11.4 0.2 copy.29
  11.6 0.2 fusion.16
  11.8 123.8 %all-gather.3.cloned.1.call-done = bf16[2,3072,384]{2,1,0:T(8,128)(2,1)} async-done(((bf16[2,48,384]{2,1,0:T(8,128)(2,1)}), bf16[2,3072,384]{2,1,0:T(8,128)(2,1)}) %all-gather.3.cloned.1.call-update) | async-done | bytes 4718608 | tf_op jit(solution)/shard_map/all_gather | solution.py:18
  135.6 4.7 %convert_add_fusion = f32[2,3072,384]{2,1,0:T(8,128)S(1)} fusion(bf16[2,3072,384]{2,1,0:T(8,128)(2,1)} %all-gather.3.cloned.1.call-done, bf16[2,3072,384]{2,1,0:T(8,128)(2,1)} %param.9), kind=kLoop, calls=%fused_computation.1 | loop fusion | flops 7077888 | bytes 18874368 | tf_op jit(solution)/shard_map/add | solution.py:27
  140.3 4.2 %fusion.22 = (f32[1,3072,384]{2,1,0:T(8,128)}, f32[1,3072,384]{2,1,0:T(8,128)}) fusion(f32[2,3072,384]{2,1,0:T(8,128)S(1)} %convert_add_fusion), kind=kLoop, calls=%fused_computation.31 | loop fusion | bytes 18874368 | tf_op jit(solution)/shard_map/slice | solution.py:45
  144.5 6.1 %copy.16 = f32[1,3072,384]{1,2,0:T(8,128)} copy(f32[1,3072,384]{2,1,0:T(8,128)} %get-tuple-element.6) | data formatting | bytes 9437184 | tf_op jit(solution)/shard_map/slice | solution.py:29
  150.7 6.1 %copy.21 = f32[1,3072,384]{1,2,0:T(8,128)} copy(f32[1,3072,384]{2,1,0:T(8,128)} %get-tuple-element.5) | data formatting | bytes 9437184 | tf_op jit(solution)/shard_map/slice | solution.py:45
  156.8 4.4 %convolution_bitcast_fusion = f32[3,48,3072]{2,1,0:T(8,128)S(1)} fusion(f32[3072,3,128]{0,2,1:T(8,128)} %bitcast.44, bf16[48,384]{1,0:T(8,128)(2,1)S(1)} %copy-done), kind=kOutput, calls=%fused_computation.5 | convolution fusion | flops 679477248 | bytes 6524928 | tf_op jit(solution)/shard_map/thd,khd->htk/dot_general | solution.py:28
  161.2 0.7 convert_reduce_fusion
  161.9 0.2 convolution_bitcast_fusion.2
  162.1 2.9 fusion.8
  165.0 89.8 %all-gather.5.cloned.1.call-done = bf16[384,3072]{0,1:T(8,128)(2,1)} async-done(((bf16[384,48]{0,1:T(8,128)(2,1)}), bf16[384,3072]{0,1:T(8,128)(2,1)}) %all-gather.5.cloned.1.call-update) | async-done | bytes 2359312 | tf_op jit(solution)/shard_map/all_gather | solution.py:55
  254.8 3.3 fusion.12
  258.1 109.5 %reduce-scatter.2.cloned.1.call-done = f32[48,384]{1,0:T(8,128)} async-done(((f32[48,3072]{1,0:T(8,128)}), f32[48,384]{1,0:T(8,128)}) %reduce-scatter.2.cloned.1.call-update) | async-done | bytes 73744 | tf_op jit(solution)/shard_map/reduce_scatter | solution.py:58
  367.6 1.5 multiply_convert_fusion.1
  (15 shorter events, 0.1 us)
Async XLA Ops:
  6.5 5.1 %copy-start = (bf16[48,384]{1,0:T(8,128)(2,1)S(1)}, bf16[48,384]{1,0:T(8,128)(2,1)}, u32[]{:S(2)}) copy-start(bf16[48,384]{1,0:T(8,128)(2,1)} %param.8) | copy-start | bytes 110596
  6.5 129.1 %all-gather.3.cloned.1.call-start = ((), (), s32[]{:S(2)}) async-start(), calls=%async_computation.1 | async-start | bytes 4792320 | tf_op jit(solution)/shard_map/all_gather | solution.py:18
  9.2 245.6 %all-gather.5.cloned.1.call-start = ((), (), s32[]{:S(2)}) async-start(), calls=%async_computation.2 | async-start | bytes 2396160 | tf_op jit(solution)/shard_map/all_gather | solution.py:55
  10.0 357.7 %reduce-scatter.2.cloned.1.call-start = ((), (), s32[]{:S(2)}) async-start(), calls=%async_computation.3 | async-start | bytes 663552 | tf_op jit(solution)/shard_map/reduce_scatter | solution.py:58
  156.8 5.4 %slice-start = ((s8[4718592]{0:T(1024)(128)(4,1)}), s8[4194304]{0:T(1024)(128)(4,1)S(1)}, s32[]{:S(2)}) async-start(s8[4718592]{0:T(1024)(128)(4,1)} %bitcast.41), calls=%async_computation.4 | async-start | bytes 8388608
  156.8 5.4 %slice-start.1 = ((s8[4718592]{0:T(1024)(128)(4,1)}), s8[524288]{0:T(1024)(128)(4,1)S(1)}, s32[]{:S(2)}) async-start(s8[4718592]{0:T(1024)(128)(4,1)} %bitcast.41), calls=%async_computation.5 | async-start | bytes 1048576
  162.1 205.5 %copy-start.1 = (f32[384]{0:T(512)S(1)}, f32[384]{0:T(512)}, u32[]{:S(2)}) copy-start(f32[384]{0:T(512)} %param.14) | copy-start | bytes 4612
  162.1 205.5 %copy-start.2 = (f32[384]{0:T(512)S(1)}, f32[384]{0:T(512)}, u32[]{:S(2)}) copy-start(f32[384]{0:T(512)} %param.15) | copy-start | bytes 4612
Sparse Core Ops, SparseCore 0:
  9.5 126.1 all-gather.2
  137.8 116.9 all-gather.4
  259.3 108.2 reduce-scatter.1
where the time goes:
time: 376 us
  waiting for transfers between devices  324 us (86%)
  local copies, waits for them, and re-layouts  18.4 us (5%)
  between operations  13.2 us (4%)
  matrix products  11 us (3%)
  other arithmetic  9.17 us (2%)
    all_gather x1, waiting for transfers between devices, body(): arrived = lax.all_gather(decoded, 'patch', axis=1, tiled=True)  124 us
    reduce_scatter x1, waiting for transfers between devices, body(): lax.psum_scatter(partial_terms, 'head', scatter_dimension=1, tiled=True)  109 us
    all_gather x1, waiting for transfers between devices, body(): lax.all_gather(out_weight, 'patch', axis=1, tiled=True)  89.8 us
    slice x2, local copies, waits for them, and re-layouts, body(): rebuilt[1]  10.3 us
  transfers between devices with their start and end apart: 3, of which 3 were waited for; matrix products, arithmetic and copies ran while one was open for 8% of the time, Pallas kernels for 0%

commit v1 on v0

v1 whole, which is shorter than its diff:
```python
import functools

import jax
import jax.numpy as jnp
from jax import lax
from jax.experimental import pallas as pl
from jax.experimental.pallas import tpu as pltpu
from jax.sharding import PartitionSpec as P

HD = 128
NX, NZ, NC, NY, NH = 4, 8, 2, 4, 2
BF = jnp.bfloat16
F32 = jnp.float32
NT = (((1,), (1,)), ((), ()))
NN = (((1,), (0,)), ((), ()))


def kernel(
    q_hbm, stale_hbm, codes_hbm, exps_hbm, text_hbm, w_hbm, bias_hbm, gate_hbm,
    out_ref,
    codes_v, exps_v, bias_v, gate_v, stale_v, text_v,
    q_all, kv, wt, o_send, o_recv, p_send, p_recv, z_send, z_recv,
    lsem, q_s, q_r, kv_s, kv_r, cf_s, cf_r, w1_s, w1_r, w2_s, w2_r, w3_s, w3_r,
    o_s, o_r, p_s, p_r, zz_s, zz_r,
):
    rows = q_hbm.shape[0]
    heads = q_hbm.shape[1] // HD
    width = q_hbm.shape[1]
    parts = NX * 2
    text_rows = text_hbm.shape[1] // parts
    p = lax.axis_index("patch")
    hd = lax.axis_index("head")
    x = lax.div(p, NZ * NC)
    z = lax.rem(lax.div(p, NC), NZ)
    c = lax.rem(p, NC)
    y = lax.div(hd, NH)
    zh = lax.rem(hd, NH)
    zi = lax.div(z, 2)
    par = lax.rem(z, 2)
    part = x * 2 + par

    def dev(xx=x, z_=z, cc=c, yy=y, hh=zh):
        return (xx * (NZ * NC) + z_ * NC + cc, yy * NH + hh)

    def up(v, k, n):
        return lax.rem(v + k, n)

    core_peer = dev(cc=1 - c)
    zh_peer = dev(hh=1 - zh)
    x_peers = [dev(xx=up(x, k, NX)) for k in (1, 2, 3)]
    y_peers = [dev(yy=up(y, k, NY)) for k in (1, 2, 3)]
    z_peers = [dev(z_=up(z, k, NZ)) for k in range(1, NZ)]
    zi_peers = [dev(z_=up(zi, k, 4) * 2 + par) for k in (1, 2, 3)]
    zx = zi * 2 + 1 - par
    pair_peers = [dev(xx=up(x, k, NX), z_=zx) for k in range(NX)]
    group = [(dev(xx=up(x, k, NX)), up(x, k, NX) * 2 + par, up(x, NX - k, NX) * 2 + par) for k in (1, 2, 3)]
    group += [(pair_peers[k], up(x, k, NX) * 2 + 1 - par, up(x, NX - k, NX) * 2 + 1 - par) for k in range(NX)]

    def remote(src, dst, s, r, to):
        return pltpu.make_async_remote_copy(
            src_ref=src, dst_ref=dst, send_sem=s, recv_sem=r, device_id=to, device_id_type=pl.DeviceIdType.MESH
        )

    barrier = pltpu.get_barrier_semaphore()
    everyone = [core_peer, zh_peer] + x_peers + y_peers + z_peers + pair_peers[1:]
    for peer in everyone:
        pl.semaphore_signal(barrier, inc=1, device_id=peer, device_id_type=pl.DeviceIdType.MESH)

    ld_codes = pltpu.make_async_copy(codes_hbm, codes_v, lsem.at[0])
    ld_exps = pltpu.make_async_copy(exps_hbm, exps_v, lsem.at[1])
    ld_w = pltpu.make_async_copy(w_hbm, wt.at[x, z, c], lsem.at[2])
    ld_q = pltpu.make_async_copy(q_hbm, q_all.at[part], lsem.at[3])
    ld_text = pltpu.make_async_copy(text_hbm.at[:, pl.ds(part * text_rows, text_rows)], text_v, lsem.at[4])
    ld_bias = pltpu.make_async_copy(bias_hbm, bias_v, lsem.at[5])
    ld_gate = pltpu.make_async_copy(gate_hbm, gate_v, lsem.at[6])
    ld_stale = [
        pltpu.make_async_copy(
            stale_hbm.at[:, pl.ds((x * (NZ * NC) + (2 * k + par) * NC) * rows, NC * rows)], stale_v.at[:, k], lsem.at[7 + k]
        )
        for k in range(4)
    ]
    loads = [ld_codes, ld_exps, ld_w, ld_q, ld_text, ld_bias, ld_gate] + ld_stale
    for ld in loads:
        ld.start()

    mine = zi * NC + c
    diagonal = lax.broadcasted_iota(jnp.int32, (rows, rows), 0) == lax.broadcasted_iota(jnp.int32, (rows, rows), 1)
    ones = jnp.ones((rows, HD), BF)
    ld_codes.wait()
    ld_exps.wait()
    for h in range(heads):
        code = codes_v[:, :, h * HD : (h + 1) * HD]
        for kind in range(2):
            step = jnp.left_shift(jnp.int32(1), exps_v[h, kind : kind + 1] + 9).astype(F32) * (2.0**-9)
            spread = jnp.where(diagonal, step, 0.0).astype(BF)
            step = lax.dot_general(spread, ones, NN, preferred_element_type=F32)
            kv[h, kind, mine] = (code[kind].astype(F32) * step).astype(BF)
    ld_w.wait()
    ld_q.wait()

    pl.semaphore_wait(barrier, len(everyone))

    pending = []

    def go(cp):
        cp.start()
        pending.append(cp)

    def send_kv(h):
        for k in (1, 2, 3):
            go(remote(kv.at[h, :, mine], kv.at[h, :, mine], kv_s.at[h, k - 1], kv_r.at[h, zi], zi_peers[k - 1]))

    send_kv(0)
    for k, (to, _, _) in enumerate(group):
        go(remote(q_all.at[part], q_all.at[part], q_s.at[k], q_r.at[part], to))
    go(remote(kv.at[:, :, mine], kv.at[:, :, mine], cf_s.at[0, 3], cf_r.at[0, 3], core_peer))
    for h in range(1, heads):
        send_kv(h)
    for k in range(1, NZ):
        go(remote(wt.at[x, z, c], wt.at[x, z, c], w1_s.at[k - 1], w1_r.at[z], z_peers[k - 1]))

    def pass_on(h):
        for k in (1, 2, 3):
            frm = up(zi, 4 - k, 4)
            slot = kv.at[h, :, frm * NC + c]
            remote(slot, slot, kv_s.at[h, k - 1], kv_r.at[h, frm], core_peer).wait_recv()
            go(remote(slot, slot, cf_s.at[h, k - 1], cf_r.at[h, k - 1], core_peer))

    def wait_core(h):
        for k in (1, 2, 3):
            slot = kv.at[h, :, up(zi, 4 - k, 4) * NC + 1 - c]
            remote(slot, slot, cf_s.at[h, k - 1], cf_r.at[h, k - 1], core_peer).wait_recv()

    scale = HD**-0.5
    tokens = parts * rows
    lane = lax.broadcasted_iota(jnp.int32, (tokens, HD), 1)
    stats = jnp.zeros((tokens, HD), F32)

    def attend(h, stats):
        cut = slice(h * HD, (h + 1) * HD)
        q = q_all[:, :, cut].reshape(tokens, HD)
        k_img = jnp.concatenate([stale_v[0, :, :, cut].reshape(tokens, HD), kv[h, 0].reshape(tokens, HD)], axis=1)
        v_img = jnp.concatenate([stale_v[1, :, :, cut].reshape(tokens, HD), kv[h, 1].reshape(tokens, HD)], axis=1)
        s_img = lax.dot_general(jnp.concatenate([q, q], axis=1), k_img, NT, preferred_element_type=F32)
        s_txt = lax.dot_general(q, text_v[0, :, cut], NT, preferred_element_type=F32)
        peak = jnp.maximum(jnp.max(s_img, axis=1, keepdims=True), jnp.max(s_txt, axis=1, keepdims=True))
        w_img = jnp.exp((s_img - peak) * scale).astype(BF)
        w_txt = jnp.exp((s_txt - peak) * scale).astype(BF)
        total = jnp.sum(w_img.astype(F32), axis=1, keepdims=True) + jnp.sum(w_txt.astype(F32), axis=1, keepdims=True)
        o_img = lax.dot_general(w_img, v_img, NN, preferred_element_type=F32)
        o_txt = lax.dot_general(w_txt, text_v[1, :, cut], NN, preferred_element_type=F32)
        o = (o_img[:, :HD] + o_img[:, HD:] + o_txt) / total
        o_send[:, h] = o.astype(BF).reshape(parts, rows, HD)
        stats = jnp.where(lax.div(lane, 3) == 2 * h, peak, stats)
        stats = jnp.where(lax.div(lane, 3) == 2 * h + 1, total, stats)
        return stats

    def send_o(h):
        span = pl.ds(h, 1 if h < heads - 1 else 2)
        for k, (to, slot, _) in enumerate(group):
            go(remote(o_send.at[slot, span], o_recv.at[part, span], o_s.at[h, k], o_r.at[h, part], to))

    pass_on(0)
    for k, (_, _, frm) in enumerate(group):
        remote(q_all.at[frm], q_all.at[frm], q_s.at[k], q_r.at[frm], core_peer).wait_recv()
    for ld in [ld_text, ld_bias, ld_gate] + ld_stale:
        ld.wait()
    other = kv.at[:, :, zi * NC + 1 - c]
    remote(other, other, cf_s.at[0, 3], cf_r.at[0, 3], core_peer).wait_recv()
    pass_on(1)
    wait_core(0)
    stats = attend(0, stats)
    send_o(0)
    pass_on(2)
    wait_core(1)
    stats = attend(1, stats)
    send_o(1)
    wait_core(2)
    stats = attend(2, stats)
    third = lax.rem(lane, 3)
    top = stats.astype(BF).astype(F32)
    mid = (stats - top).astype(BF).astype(F32)
    low = stats - top - mid
    o_send[:, heads] = jnp.where(third == 0, top, jnp.where(third == 1, mid, low)).astype(BF).reshape(parts, rows, HD)
    send_o(2)

    for k in range(1, NZ):
        frm = up(z, NZ - k, NZ)
        remote(wt.at[x, frm, c], wt.at[x, frm, c], w1_s.at[k - 1], w1_r.at[frm], core_peer).wait_recv()
    for k in (1, 2, 3):
        go(remote(wt.at[x, :, c], wt.at[x, :, c], w2_s.at[k - 1], w2_r.at[x], x_peers[k - 1]))

    o_recv[part] = o_send[part]
    for h in range(heads):
        span = pl.ds(h, 1 if h < heads - 1 else 2)
        for k, (_, _, frm) in enumerate(group):
            slot = o_recv.at[frm, span]
            remote(slot, slot, o_s.at[h, k], o_r.at[h, frm], core_peer).wait_recv()
    pick_row = lax.broadcasted_iota(jnp.int32, (HD, 2 * heads * HD), 0)
    pick_col = lax.broadcasted_iota(jnp.int32, (HD, 2 * heads * HD), 1)
    pick = (lax.div(pick_row, 3) == lax.div(pick_col, HD)).astype(F32).astype(BF)
    wide = lax.dot_general(o_recv[:, heads].reshape(tokens, HD), pick, NN, preferred_element_type=F32)
    wide = wide.reshape(parts, rows, 2 * heads * HD)
    cols = []
    for h in range(heads):
        peak = wide[:, :, 2 * h * HD : (2 * h + 1) * HD]
        total = wide[:, :, (2 * h + 1) * HD : (2 * h + 2) * HD]
        share = jnp.exp((peak - jnp.max(peak, axis=0, keepdims=True)) * scale) * total
        mix = jnp.sum(share * o_recv[:, h].astype(F32), axis=0) / jnp.sum(share, axis=0)
        cols.append(mix.astype(BF))
    attended = jnp.concatenate(cols, axis=1)

    for k in (1, 2, 3):
        frm = up(x, NX - k, NX)
        remote(wt.at[frm, :, c], wt.at[frm, :, c], w2_s.at[k - 1], w2_r.at[frm], core_peer).wait_recv()
    go(remote(wt.at[:, :, c], wt.at[:, :, c], w3_s, w3_r, core_peer))
    remote(wt.at[:, :, 1 - c], wt.at[:, :, 1 - c], w3_s, w3_r, core_peer).wait_recv()

    own = []
    for half in range(2):
        hh = (1 - zh) if half == 0 else zh
        for k in (1, 2, 3, 0):
            yy = up(y, k, NY)
            block = wt[yy, pl.ds(hh * 4, 4)].reshape(width, width)
            term = lax.dot_general(attended, block, NT, preferred_element_type=F32)
            if k:
                p_send[half, k - 1] = term.astype(BF)
                go(remote(p_send.at[half, k - 1], p_recv.at[half, y], p_s.at[half, k - 1], p_r.at[half, y], y_peers[k - 1]))
            else:
                own.append(term)

    def gather(half):
        acc = own[half]
        for k in (1, 2, 3):
            frm = up(y, NY - k, NY)
            slot = p_recv.at[half, frm]
            remote(slot, slot, p_s.at[half, k - 1], p_r.at[half, frm], core_peer).wait_recv()
            acc = acc + p_recv[half, frm].astype(F32)
        return acc

    z_send[...] = gather(0).astype(BF)
    go(remote(z_send, z_recv, zz_s, zz_r, zh_peer))
    near = gather(1) + bias_v[...].reshape(1, width)
    remote(z_send, z_recv, zz_s, zz_r, zh_peer).wait_recv()
    out_ref[...] = (gate_v[...].reshape(1, width) * (near + z_recv[...].astype(F32))).astype(BF)
    for cp in pending:
        cp.wait_send()


def body(queries, stale_kv, codes, exponents, text_kv, out_weight, out_bias, out_gate):
    rows, width = queries.shape
    heads = width // HD
    parts = NX * 2
    dma = pltpu.SemaphoreType.DMA
    any_spec = pl.BlockSpec(memory_space=pl.ANY)
    return pl.pallas_call(
        kernel,
        out_shape=jax.ShapeDtypeStruct((rows, width), BF),
        in_specs=[any_spec] * 8,
        out_specs=pl.BlockSpec(memory_space=pltpu.VMEM),
        scratch_shapes=[
            pltpu.VMEM(codes.shape, jnp.int32),
            pltpu.VMEM((heads, 2, rows), jnp.int32),
            pltpu.VMEM((width,), F32),
            pltpu.VMEM((width,), F32),
            pltpu.VMEM((2, 4, NC * rows, width), BF),
            pltpu.VMEM((2, text_kv.shape[1] // parts, width), BF),
            pltpu.VMEM((parts, rows, width), BF),
            pltpu.VMEM((heads, 2, 8, rows, HD), BF),
            pltpu.VMEM((NX, NZ, NC, rows, width), BF),
            pltpu.VMEM((parts, heads + 1, rows, HD), BF),
            pltpu.VMEM((parts, heads + 1, rows, HD), BF),
            pltpu.VMEM((2, 3, rows, width), BF),
            pltpu.VMEM((2, NY, rows, width), BF),
            pltpu.VMEM((rows, width), BF),
            pltpu.VMEM((rows, width), BF),
            dma((11,)),
            dma((7,)), dma((parts,)),
            dma((heads, 3)), dma((heads, 4)),
            dma((heads, 4)), dma((heads, 4)),
            dma((7,)), dma((NZ,)),
            dma((3,)), dma((NX,)),
            dma(()), dma(()),
            dma((heads, 7)), dma((heads, parts)),
            dma((2, 3)), dma((2, NY)),
            dma(()), dma(()),
        ],
        compiler_params=pltpu.CompilerParams(
            collective_id=0, has_side_effects=True, vmem_limit_bytes=60 * 1024 * 1024
        ),
        cost_estimate=pl.CostEstimate(flops=640_000_000, bytes_accessed=4_000_000, transcendentals=520_000),
        name="joint_attention",
    )(
        queries, stale_kv, codes, exponents.transpose(2, 0, 1), text_kv, out_weight.T,
        out_bias, out_gate,
    )


def solution(mesh):
    placed = (
        P("patch", "head"),
        P(None, None, "head"),
        P(None, "patch", "head"),
        P(None, "patch", "head"),
        P(None, None, "head"),
        P("head", "patch"),
        P("head"),
        P("head"),
    )
    return jax.shard_map(
        body, mesh=mesh, in_specs=placed, out_specs=P("patch", "head"), check_vma=False
    )
```

time: 376 us -> 77.4 us (0.21)
  the two profiles are of different devices: /device:TPU:6 before, /device:TPU:32 now
where the time goes in v1:
time: 77.4 us; the launch traced here: 77.2 us
  Pallas kernels  75.8 us (98%)
  local copies, waits for them, and re-layouts  1.39 us (2%)
    pallas_call x1, Pallas kernels, body(): pl.pallas_call(kernel, out_shape=jax.ShapeDtypeStruct((rows, width), BF),...  75.8 us

profile of v1, /device:TPU:32, one launch (start us, length us, event | category | flops | bytes accessed | tf_op | source)
XLA Modules:
  0.0 77.2 jit_solution(289148627248111316)
XLA Ops:
  0.0 75.8 %joint_attention.1 = bf16[48,384]{1,0:T(8,128)(2,1)} custom-call(bf16[48,384]{1,0:T(8,128)(2,1)} %q_hbm.1, bf16[2,3072,384]{2,1,0:T(8,128)(2,1)} %stale_hbm.1, s32[2,48,384]{2,1,0:T(8,128)} %codes_hbm.1, s32[3,2,48]{2,1,0:T(2,128)} %bitcast.3, bf16[2,512,384]{2,1,0:T(8,128)(2,1)} %text_hbm.1, bf16[48,384]{1,0:T(8,128)(2,1)} %bitcast.2, f32[384]{0:T(512)} %bias_hbm.1, ...), custom_call_target="tpu_custom_call" | custom-call | flops 640000000 | bytes 4000000 | tf_op jit(solution)/shard_map/joint_attention/pallas_call | solution.py:256
  75.8 1.4 %copy.10 = bf16[48,384]{1,0:T(8,128)(2,1)} copy(bf16[48,384]{1,0:T(8,128)(2,1)} %joint_attention.1) | data formatting | bytes 73728

commit v2 on v1

v2 whole, which is shorter than its diff:
```python
import jax
import jax.numpy as jnp
from jax import lax
from jax.experimental import pallas as pl
from jax.experimental.pallas import tpu as pltpu
from jax.sharding import PartitionSpec as P

HD = 128
NX, NZ, NC, NY, NH = 4, 8, 2, 4, 2
QUAD = 4
BF = jnp.bfloat16
F32 = jnp.float32
MESH = pl.DeviceIdType.MESH
NT = (((1,), (1,)), ((), ()))
NN = (((1,), (0,)), ((), ()))


def kernel(
    q_hbm, stale_hbm, codes_hbm, exps_hbm, text_hbm, w_hbm, bias_hbm, gate_hbm,
    out_ref,
    codes_v, exps_v, bias_v, gate_v, stale_v, text_v,
    q_all, kv, wt, o_send, o_recv, p_send, p_recv, z_send, z_recv,
    lsem, q_s, q_r, kh_s, kh_r, kx_s, kx_r, kf_s, kf_r, kc_s, kc_r,
    wh_s, wh_r, wq_s, wq_r, wx_s, wx_r, wf_s, wf_r, wc_s, wc_r,
    o_s, o_r, p_s, p_r, zz_s, zz_r, entered,
):
    rows, width = q_hbm.shape
    heads = width // HD
    text_rows = text_hbm.shape[1] // QUAD
    p = lax.axis_index("patch")
    hd = lax.axis_index("head")
    x = lax.div(p, NZ * NC)
    z = lax.rem(lax.div(p, NC), NZ)
    c = lax.rem(p, NC)
    y = lax.div(hd, NH)
    zh = lax.rem(hd, NH)
    zb = lax.div(z, QUAD)
    zq = lax.rem(z, QUAD)

    def dev(xx=x, z_=z, cc=c, yy=y, hh=zh):
        return (xx * (NZ * NC) + z_ * NC + cc, yy * NH + hh)

    def ring(k):
        at = lax.rem(zh * NZ + z + k, NZ * NH)
        return dev(z_=lax.rem(at, NZ), hh=lax.div(at, NZ))

    core_peer = dev(cc=1 - c)
    half_peer = dev(z_=(1 - zb) * QUAD + zq)
    zh_peer = dev(hh=1 - zh)
    x_at = [lax.rem(x + k, NX) for k in (1, 2, 3)]
    y_at = [lax.rem(y + k, NY) for k in (1, 2, 3)]
    q_at = [lax.rem(zq + k, QUAD) for k in (1, 2, 3)]
    x_peers = [dev(xx=v) for v in x_at]
    y_peers = [dev(yy=v) for v in y_at]
    q_peers = [dev(z_=zb * QUAD + v) for v in q_at]

    pending = []

    def send(src, dst, s, r, to):
        cp = pltpu.make_async_remote_copy(
            src_ref=src, dst_ref=dst, send_sem=s, recv_sem=r, device_id=to, device_id_type=MESH
        )
        cp.start()
        pending.append(cp)

    def arrive(dst, s, r):
        pltpu.make_async_remote_copy(
            src_ref=dst, dst_ref=dst, send_sem=s, recv_sem=r, device_id=core_peer, device_id_type=MESH
        ).wait_recv()

    barrier = pltpu.get_barrier_semaphore()
    everyone = [ring(4), ring(NZ * NH - 4), core_peer] + x_peers + y_peers + q_peers
    for peer in everyone:
        pl.semaphore_signal(barrier, inc=1, device_id=peer, device_id_type=MESH)

    ld_codes = pltpu.make_async_copy(codes_hbm, codes_v, lsem.at[0])
    ld_exps = pltpu.make_async_copy(exps_hbm, exps_v, lsem.at[1])
    ld_w = pltpu.make_async_copy(w_hbm, wt.at[zb, x, 0, c], lsem.at[2])
    ld_q = pltpu.make_async_copy(q_hbm, q_all.at[zq], lsem.at[3])
    ld_text = pltpu.make_async_copy(text_hbm.at[:, pl.ds(zq * text_rows, text_rows)], text_v, lsem.at[4])
    ld_bias = pltpu.make_async_copy(bias_hbm, bias_v, lsem.at[5])
    ld_gate = pltpu.make_async_copy(gate_hbm, gate_v, lsem.at[6])
    ld_stale = [
        pltpu.make_async_copy(
            stale_hbm.at[:, pl.ds((xx * NZ + b * QUAD + zq) * NC * rows, NC * rows)],
            stale_v.at[:, xx, b], lsem.at[7 + xx * 2 + b],
        )
        for xx in range(NX) for b in range(2)
    ]
    for ld in [ld_codes, ld_exps, ld_w, ld_q, ld_text, ld_bias, ld_gate] + ld_stale:
        ld.start()

    diagonal = lax.broadcasted_iota(jnp.int32, (rows, rows), 0) == lax.broadcasted_iota(jnp.int32, (rows, rows), 1)
    ones = jnp.ones((rows, HD), BF)
    ld_codes.wait()
    ld_exps.wait()
    for h in range(heads):
        code = codes_v[:, :, h * HD : (h + 1) * HD]
        for kind in range(2):
            step = jnp.left_shift(jnp.int32(1), exps_v[h, kind : kind + 1] + 9).astype(F32) * (2.0**-9)
            spread = jnp.where(diagonal, step, 0.0).astype(BF)
            step = lax.dot_general(spread, ones, NN, preferred_element_type=F32)
            kv[h, kind, x, zb, c] = (code[kind].astype(F32) * step).astype(BF)
    ld_w.wait()
    ld_q.wait()

    pl.semaphore_wait(barrier, len(everyone))
    pl.semaphore_signal(entered, inc=1, device_id=ring(4), device_id_type=MESH)

    def send_half(h):
        mine = kv.at[h, :, x, zb, c]
        send(mine, mine, kh_s.at[h], kh_r.at[h], half_peer)

    send_half(0)
    for k in range(3):
        send(q_all.at[zq], q_all.at[zq], q_s.at[k], q_r.at[zq], q_peers[k])
    for h in range(1, heads):
        send_half(h)
    for k in range(3):
        mine = kv.at[:, :, x, zb, c]
        send(mine, mine, kx_s.at[k], kx_r.at[x], x_peers[k])
    own_w = wt.at[zb, x, 0, c]
    send(own_w, own_w, wh_s, wh_r, half_peer)
    for k in range(3):
        send(own_w, wt.at[zb, x, 3 - k, c], wq_s.at[0, k], wq_r.at[0, 3 - k], q_peers[k])
    for k in range(3):
        send(own_w, own_w, wx_s.at[0, k], wx_r.at[0, x], x_peers[k])

    def from_x(h):
        for k in range(3):
            slot = kv.at[h, :, x_at[k], 1 - zb, c]
            arrive(slot, kf_s.at[h, k], kf_r.at[h, x_at[k]])
        slot = kv.at[h, :, :, 1 - zb, c]
        send(slot, slot, kc_s.at[1 + h], kc_r.at[1 + h], core_peer)

    def from_core(h):
        slot = kv.at[h, :, :, 1 - zb, 1 - c]
        arrive(slot, kc_s.at[1 + h], kc_r.at[1 + h])

    scale = HD**-0.5
    tokens = QUAD * rows
    keys = NX * 2 * NC * rows
    lane = lax.broadcasted_iota(jnp.int32, (tokens, HD), 1)

    def attend(h, stats):
        cut = slice(h * HD, (h + 1) * HD)
        q = q_all[:, :, cut].reshape(tokens, HD)
        k_img = jnp.concatenate([stale_v[0, :, :, :, cut].reshape(keys, HD), kv[h, 0].reshape(keys, HD)], axis=1)
        v_img = jnp.concatenate([stale_v[1, :, :, :, cut].reshape(keys, HD), kv[h, 1].reshape(keys, HD)], axis=1)
        s_img = lax.dot_general(jnp.concatenate([q, q], axis=1), k_img, NT, preferred_element_type=F32)
        s_txt = lax.dot_general(q, text_v[0, :, cut], NT, preferred_element_type=F32)
        peak = jnp.maximum(jnp.max(s_img, axis=1, keepdims=True), jnp.max(s_txt, axis=1, keepdims=True))
        w_img = jnp.exp((s_img - peak) * scale).astype(BF)
        w_txt = jnp.exp((s_txt - peak) * scale).astype(BF)
        total = jnp.sum(w_img.astype(F32), axis=1, keepdims=True) + jnp.sum(w_txt.astype(F32), axis=1, keepdims=True)
        o_img = lax.dot_general(w_img, v_img, NN, preferred_element_type=F32)
        o_txt = lax.dot_general(w_txt, text_v[1, :, cut], NN, preferred_element_type=F32)
        o = (o_img[:, :HD] + o_img[:, HD:] + o_txt) / total
        o_send[:, h] = o.astype(BF).reshape(QUAD, rows, HD)
        stats = jnp.where(lax.div(lane, 3) == 2 * h, peak, stats)
        stats = jnp.where(lax.div(lane, 3) == 2 * h + 1, total, stats)
        return stats

    def send_o(h):
        span = pl.ds(h, 1 if h < heads - 1 else 2)
        for k in range(3):
            send(o_send.at[q_at[k], span], o_recv.at[zq, span], o_s.at[h, k], o_r.at[h, zq], q_peers[k])

    for h in range(heads):
        slot = kv.at[h, :, x, 1 - zb, c]
        arrive(slot, kh_s.at[h], kh_r.at[h])
        for k in range(3):
            send(slot, slot, kf_s.at[h, k], kf_r.at[h, x], x_peers[k])
        if h == 0:
            for k in range(3):
                there = kv.at[:, :, x_at[k], zb, c]
                arrive(there, kx_s.at[k], kx_r.at[x_at[k]])
            all_x = kv.at[:, :, :, zb, c]
            send(all_x, all_x, kc_s.at[0], kc_r.at[0], core_peer)
    half_w = wt.at[1 - zb, x, 0, c]
    arrive(half_w, wh_s, wh_r)
    for k in range(3):
        send(half_w, wt.at[1 - zb, x, 3 - k, c], wq_s.at[1, k], wq_r.at[1, 3 - k], q_peers[k])
    for k in range(3):
        send(half_w, half_w, wx_s.at[1, k], wx_r.at[1, x], x_peers[k])

    def spread_w(b, side):
        for k in range(3):
            arrive(wt.at[side, x, k + 1, c], wq_s.at[b, k], wq_r.at[b, k + 1])
        rest = wt.at[side, x, pl.ds(1, 3), c]
        for k in range(3):
            send(rest, rest, wf_s.at[b, k], wf_r.at[b, x], x_peers[k])

    def cross_w(b, side):
        for k in range(3):
            arrive(wt.at[side, x_at[k], 0, c], wx_s.at[b, k], wx_r.at[b, x_at[k]])
            arrive(wt.at[side, x_at[k], pl.ds(1, 3), c], wf_s.at[b, k], wf_r.at[b, x_at[k]])
        mine = wt.at[side, :, :, c]
        send(mine, mine, wc_s.at[b], wc_r.at[side], core_peer)

    for k in range(3):
        arrive(q_all.at[q_at[k]], q_s.at[k], q_r.at[q_at[k]])
    for ld in [ld_text, ld_bias, ld_gate] + ld_stale:
        ld.wait()
    from_x(0)
    spread_w(0, zb)
    from_x(1)
    all_x = kv.at[:, :, :, zb, 1 - c]
    arrive(all_x, kc_s.at[0], kc_r.at[0])
    from_core(0)
    stats = attend(0, jnp.zeros((tokens, HD), F32))
    send_o(0)
    from_x(2)
    from_core(1)
    stats = attend(1, stats)
    send_o(1)
    from_core(2)
    stats = attend(2, stats)
    third = lax.rem(lane, 3)
    top = stats.astype(BF).astype(F32)
    mid = (stats - top).astype(BF).astype(F32)
    low = stats - top - mid
    o_send[:, heads] = jnp.where(third == 0, top, jnp.where(third == 1, mid, low)).astype(BF).reshape(QUAD, rows, HD)
    send_o(2)
    spread_w(1, 1 - zb)
    cross_w(0, zb)

    o_recv[zq] = o_send[zq]

    def from_quad(h):
        span = pl.ds(h, 1 if h < heads - 1 else 2)
        for k in range(3):
            arrive(o_recv.at[q_at[k], span], o_s.at[h, k], o_r.at[h, q_at[k]])

    from_quad(0)
    from_quad(1)
    from_quad(2)
    pick_row = lax.broadcasted_iota(jnp.int32, (HD, 2 * heads * HD), 0)
    pick_col = lax.broadcasted_iota(jnp.int32, (HD, 2 * heads * HD), 1)
    pick = (lax.div(pick_row, 3) == lax.div(pick_col, HD)).astype(F32).astype(BF)
    wide = lax.dot_general(o_recv[:, heads].reshape(tokens, HD), pick, NN, preferred_element_type=F32)
    wide = wide.reshape(QUAD, rows, 2 * heads * HD)
    cols = []
    for h in range(heads):
        peak = wide[:, :, 2 * h * HD : (2 * h + 1) * HD]
        total = wide[:, :, (2 * h + 1) * HD : (2 * h + 2) * HD]
        share = jnp.exp((peak - jnp.max(peak, axis=0, keepdims=True)) * scale) * total
        mix = jnp.sum(share * o_recv[:, h].astype(F32), axis=0) / jnp.sum(share, axis=0)
        cols.append(mix.astype(BF))
    attended = jnp.concatenate(cols, axis=1)

    cross_w(1, 1 - zb)
    for b, side in ((0, zb), (1, 1 - zb)):
        arrive(wt.at[side, :, :, 1 - c], wc_s.at[b], wc_r.at[side])

    own = []
    for half in range(2):
        side = (1 - zh) if half == 0 else zh
        for k in (0, 1, 2, 3):
            to = y_at[k] if k < 3 else y
            pieces = [wt[side, to, lax.rem(v + QUAD - zq, QUAD)].reshape(NC * rows, width) for v in range(QUAD)]
            term = lax.dot_general(attended, jnp.concatenate(pieces, axis=0), NT, preferred_element_type=F32)
            if k < 3:
                p_send[half, k] = term.astype(BF)
                send(p_send.at[half, k], p_recv.at[half, y], p_s.at[half, k], p_r.at[half, y], y_peers[k])
            else:
                own.append(term)

    def gather(half):
        acc = own[half]
        for k in range(3):
            arrive(p_recv.at[half, y_at[k]], p_s.at[half, k], p_r.at[half, y_at[k]])
            acc = acc + p_recv[half, y_at[k]].astype(F32)
        return acc

    z_send[...] = gather(0).astype(BF)
    pl.semaphore_wait(entered, 1)
    send(z_send, z_recv, zz_s, zz_r, zh_peer)
    near = gather(1) + bias_v[...].reshape(1, width)
    arrive(z_recv, zz_s, zz_r)
    out_ref[...] = (gate_v[...].reshape(1, width) * (near + z_recv[...].astype(F32))).astype(BF)
    for cp in pending:
        cp.wait_send()


def body(queries, stale_kv, codes, exponents, text_kv, out_weight, out_bias, out_gate):
    rows, width = queries.shape
    heads = width // HD
    dma = pltpu.SemaphoreType.DMA
    any_spec = pl.BlockSpec(memory_space=pl.ANY)
    return pl.pallas_call(
        kernel,
        out_shape=jax.ShapeDtypeStruct((rows, width), BF),
        in_specs=[any_spec] * 8,
        out_specs=pl.BlockSpec(memory_space=pltpu.VMEM),
        scratch_shapes=[
            pltpu.VMEM(codes.shape, jnp.int32),
            pltpu.VMEM((heads, 2, rows), jnp.int32),
            pltpu.VMEM((width,), F32),
            pltpu.VMEM((width,), F32),
            pltpu.VMEM((2, NX, 2, NC * rows, width), BF),
            pltpu.VMEM((2, text_kv.shape[1] // QUAD, width), BF),
            pltpu.VMEM((QUAD, rows, width), BF),
            pltpu.VMEM((heads, 2, NX, 2, NC, rows, HD), BF),
            pltpu.VMEM((2, NX, QUAD, NC, rows, width), BF),
            pltpu.VMEM((QUAD, heads + 1, rows, HD), BF),
            pltpu.VMEM((QUAD, heads + 1, rows, HD), BF),
            pltpu.VMEM((2, 3, rows, width), BF),
            pltpu.VMEM((2, NY, rows, width), BF),
            pltpu.VMEM((rows, width), BF),
            pltpu.VMEM((rows, width), BF),
            dma((15,)),
            dma((3,)), dma((QUAD,)),
            dma((heads,)), dma((heads,)),
            dma((3,)), dma((NX,)),
            dma((heads, 3)), dma((heads, NX)),
            dma((heads + 1,)), dma((heads + 1,)),
            dma(()), dma(()),
            dma((2, 3)), dma((2, QUAD)),
            dma((2, 3)), dma((2, NX)),
            dma((2, 3)), dma((2, NX)),
            dma((2,)), dma((2,)),
            dma((heads, 3)), dma((heads, QUAD)),
            dma((2, 3)), dma((2, NY)),
            dma(()), dma(()),
            pltpu.SemaphoreType.REGULAR,
        ],
        compiler_params=pltpu.CompilerParams(
            collective_id=0, has_side_effects=True, vmem_limit_bytes=60 * 1024 * 1024
        ),
        cost_estimate=pl.CostEstimate(flops=640_000_000, bytes_accessed=4_000_000, transcendentals=520_000),
        name="joint_attention",
    )(
        queries, stale_kv, codes, exponents.transpose(2, 0, 1), text_kv, out_weight.T,
        out_bias, out_gate,
    )


def solution(mesh):
    placed = (
        P("patch", "head"),
        P(None, None, "head"),
        P(None, "patch", "head"),
        P(None, "patch", "head"),
        P(None, None, "head"),
        P("head", "patch"),
        P("head"),
        P("head"),
    )
    return jax.shard_map(
        body, mesh=mesh, in_specs=placed, out_specs=P("patch", "head"), check_vma=False
    )
```

time: 77.4 us -> 59.3 us (0.77)
  the two profiles are of different devices: /device:TPU:32 before, /device:TPU:65 now
where the time goes in v2:
time: 59.3 us; the launch traced here: 59.1 us
  Pallas kernels  57.7 us (97%)
  local copies, waits for them, and re-layouts  1.39 us (2%)
    pallas_call x1, Pallas kernels, body(): pl.pallas_call(kernel, out_shape=jax.ShapeDtypeStruct((rows, width), BF),...  57.7 us
    unnamed x1, local copies, waits for them, and re-layouts  1.39 us

profile of v2, /device:TPU:65, one launch (start us, length us, event | category | flops | bytes accessed | tf_op | source)
XLA Modules:
  0.0 59.1 jit_solution(13807975254230859294)
XLA Ops:
  0.0 57.7 %joint_attention.1 = bf16[48,384]{1,0:T(8,128)(2,1)} custom-call(bf16[48,384]{1,0:T(8,128)(2,1)} %q_hbm.1, bf16[2,3072,384]{2,1,0:T(8,128)(2,1)} %stale_hbm.1, s32[2,48,384]{2,1,0:T(8,128)} %codes_hbm.1, s32[3,2,48]{2,1,0:T(2,128)} %bitcast.3, bf16[2,512,384]{2,1,0:T(8,128)(2,1)} %text_hbm.1, bf16[48,384]{1,0:T(8,128)(2,1)} %bitcast.2, f32[384]{0:T(512)} %bias_hbm.1, ...), custom_call_target="tpu_custom_call" | custom-call | flops 640000000 | bytes 4000000 | tf_op jit(solution)/shard_map/joint_attention/pallas_call | solution.py:291
  57.7 1.4 %copy.10 = bf16[48,384]{1,0:T(8,128)(2,1)} copy(bf16[48,384]{1,0:T(8,128)(2,1)} %joint_attention.1) | data formatting | bytes 73728

commit v3 on v2

v3 whole, which is shorter than its diff:
```python
import jax
import jax.numpy as jnp
from jax import lax
from jax.experimental import pallas as pl
from jax.experimental.pallas import tpu as pltpu
from jax.sharding import PartitionSpec as P

HD = 128
NX, NZ, NC, NY, NH = 4, 8, 2, 4, 2
QUAD = 4
BF = jnp.bfloat16
F32 = jnp.float32
MESH = pl.DeviceIdType.MESH
NT = (((1,), (1,)), ((), ()))
NN = (((1,), (0,)), ((), ()))
TN = (((0,), (0,)), ((), ()))
STATS = 16


def kernel(
    q_hbm, stale_hbm, codes_hbm, exps_hbm, text_hbm, w_hbm, bias_hbm, gate_hbm,
    out_ref,
    codes_v, exps_v, bias_v, gate_v, stale_v, text_v,
    q_all, kv, wt, o_send, o_recv, a_all, p_send, p_recv, z_send, z_recv,
    lsem, q_s, q_r, kh_s, kh_r, kx_s, kx_r, kf_s, kf_r, kc_s, kc_r,
    wh_s, wh_r, wq_s, wq_r, wc_s, wc_r, o_s, o_r, a_s, a_r, p_s, p_r, zz_s, zz_r, entered,
):
    rows, width = q_hbm.shape
    heads = width // HD
    text_rows = text_hbm.shape[1] // QUAD
    p = lax.axis_index("patch")
    hd = lax.axis_index("head")
    x = lax.div(p, NZ * NC)
    z = lax.rem(lax.div(p, NC), NZ)
    c = lax.rem(p, NC)
    y = lax.div(hd, NH)
    zh = lax.rem(hd, NH)
    zb = lax.div(z, QUAD)
    zq = lax.rem(z, QUAD)
    far, near = 1 - zh, zh

    def dev(xx=x, z_=z, cc=c, yy=y, hh=zh):
        return (xx * (NZ * NC) + z_ * NC + cc, yy * NH + hh)

    def ring(k):
        at = lax.rem(zh * NZ + z + k, NZ * NH)
        return dev(z_=lax.rem(at, NZ), hh=lax.div(at, NZ))

    core_peer = dev(cc=1 - c)
    half_peer = dev(z_=(1 - zb) * QUAD + zq)
    zh_peer = dev(hh=1 - zh)
    x_at = [lax.rem(x + k, NX) for k in (1, 2, 3)]
    y_at = [lax.rem(y + k, NY) for k in (1, 2, 3)]
    q_at = [lax.rem(zq + k, QUAD) for k in (1, 2, 3)]
    x_peers = [dev(xx=v) for v in x_at]
    feature_peers = [dev(xx=v, yy=x) for v in x_at]
    feature_home = dev(yy=x)
    feature_from = [dev(xx=y, yy=v) for v in y_at]
    away = x != y
    feature_near = dev(xx=y, cc=jnp.where(away, c, 1 - c))
    q_peers = [dev(z_=zb * QUAD + v) for v in q_at]

    pending = []

    def send(src, dst, s, r, to):
        cp = pltpu.make_async_remote_copy(
            src_ref=src, dst_ref=dst, send_sem=s, recv_sem=r, device_id=to, device_id_type=MESH
        )
        cp.start()
        pending.append(cp)

    def arrive(dst, s, r):
        pltpu.make_async_remote_copy(
            src_ref=dst, dst_ref=dst, send_sem=s, recv_sem=r, device_id=core_peer, device_id_type=MESH
        ).wait_recv()

    barrier = pltpu.get_barrier_semaphore()
    everyone = [ring(4), ring(NZ * NH - 4), core_peer] + x_peers + q_peers
    for peer in everyone + feature_from + [feature_near]:
        pl.semaphore_signal(barrier, inc=1, device_id=peer, device_id_type=MESH)

    ld_codes = pltpu.make_async_copy(codes_hbm, codes_v, lsem.at[0])
    ld_exps = pltpu.make_async_copy(exps_hbm, exps_v, lsem.at[1])
    ld_w = pltpu.make_async_copy(w_hbm, wt.at[zb, 0, c], lsem.at[2])
    ld_q = pltpu.make_async_copy(q_hbm, q_all.at[zq], lsem.at[3])
    ld_text = pltpu.make_async_copy(text_hbm.at[:, pl.ds(zq * text_rows, text_rows)], text_v, lsem.at[4])
    ld_bias = pltpu.make_async_copy(bias_hbm, bias_v, lsem.at[5])
    ld_gate = pltpu.make_async_copy(gate_hbm, gate_v, lsem.at[6])
    ld_stale = [
        pltpu.make_async_copy(
            stale_hbm.at[:, pl.ds((xx * NZ + b * QUAD + zq) * NC * rows, NC * rows)],
            stale_v.at[:, xx, b], lsem.at[7 + xx * 2 + b],
        )
        for xx in range(NX) for b in range(2)
    ]
    for ld in [ld_codes, ld_exps, ld_w, ld_q, ld_text, ld_bias, ld_gate] + ld_stale:
        ld.start()

    diagonal = lax.broadcasted_iota(jnp.int32, (rows, rows), 0) == lax.broadcasted_iota(jnp.int32, (rows, rows), 1)
    ones = jnp.ones((rows, HD), BF)
    ld_codes.wait()
    ld_exps.wait()
    for h in range(heads):
        code = codes_v[:, :, h * HD : (h + 1) * HD]
        for kind in range(2):
            step = jnp.left_shift(jnp.int32(1), exps_v[h, kind : kind + 1] + 9).astype(F32) * (2.0**-9)
            spread = jnp.where(diagonal, step, 0.0).astype(BF)
            step = lax.dot_general(spread, ones, NN, preferred_element_type=F32)
            kv[h, kind, x, zb, c] = (code[kind].astype(F32) * step).astype(BF)
    ld_w.wait()
    ld_q.wait()

    pl.semaphore_wait(barrier, len(everyone) + 4)
    pl.semaphore_signal(entered, inc=1, device_id=ring(4), device_id_type=MESH)

    def kv_half(h):
        mine = kv.at[h, :, x, zb, c]
        send(mine, mine, kh_s.at[h], kh_r.at[h], half_peer)

    def kv_x():
        for k in range(3):
            mine = kv.at[:, :, x, zb, c]
            send(mine, mine, kx_s.at[k], kx_r.at[x], x_peers[k])

    def q_quad():
        for k in range(3):
            send(q_all.at[zq], q_all.at[zq], q_s.at[k], q_r.at[zq], q_peers[k])

    own_w = wt.at[zb, 0, c]
    half_w = wt.at[1 - zb, 0, c]

    def w_half():
        send(own_w, own_w, wh_s, wh_r, half_peer)

    def w_got_half():
        arrive(half_w, wh_s, wh_r)

    def w_quad(side):
        for k in range(3):
            send(wt.at[side, 0, c], wt.at[side, 3 - k, c], wq_s.at[side, k], wq_r.at[side, 3 - k], q_peers[k])

    def w_core(side):
        for k in range(3):
            arrive(wt.at[side, k + 1, c], wq_s.at[side, k], wq_r.at[side, k + 1])
        mine = wt.at[side, :, c]
        send(mine, mine, wc_s.at[side], wc_r.at[side], core_peer)

    def w_done(side):
        arrive(wt.at[side, :, 1 - c], wc_s.at[side], wc_r.at[side])

    def kv_on(h):
        slot = kv.at[h, :, x, 1 - zb, c]
        arrive(slot, kh_s.at[h], kh_r.at[h])
        for k in range(3):
            send(slot, slot, kf_s.at[h, k], kf_r.at[h, x], x_peers[k])

    def kv_core():
        for k in range(3):
            there = kv.at[:, :, x_at[k], zb, c]
            arrive(there, kx_s.at[k], kx_r.at[x_at[k]])
        all_x = kv.at[:, :, :, zb, c]
        send(all_x, all_x, kc_s.at[0], kc_r.at[0], core_peer)

    def kv_core_on(h):
        for k in range(3):
            slot = kv.at[h, :, x_at[k], 1 - zb, c]
            arrive(slot, kf_s.at[h, k], kf_r.at[h, x_at[k]])
        slot = kv.at[h, :, :, 1 - zb, c]
        send(slot, slot, kc_s.at[1 + h], kc_r.at[1 + h], core_peer)

    def ready():
        for k in range(3):
            arrive(q_all.at[q_at[k]], q_s.at[k], q_r.at[q_at[k]])
        for ld in [ld_text, ld_bias, ld_gate] + ld_stale:
            ld.wait()
        all_x = kv.at[:, :, :, zb, 1 - c]
        arrive(all_x, kc_s.at[0], kc_r.at[0])

    scale = HD**-0.5
    tokens = QUAD * rows
    keys = NX * 2 * NC * rows
    lane = lax.broadcasted_iota(jnp.int32, (tokens, HD), 1)
    first_row = lax.broadcasted_iota(jnp.int32, (STATS, HD), 0)
    first = (first_row == lax.broadcasted_iota(jnp.int32, (STATS, HD), 1)).astype(F32).astype(BF)

    def attend(h):
        slot = kv.at[h, :, :, 1 - zb, 1 - c]
        arrive(slot, kc_s.at[1 + h], kc_r.at[1 + h])
        cut = slice(h * HD, (h + 1) * HD)
        q = q_all[:, :, cut].reshape(tokens, HD)
        k_img = jnp.concatenate([stale_v[0, :, :, :, cut].reshape(keys, HD), kv[h, 0].reshape(keys, HD)], axis=1)
        v_img = jnp.concatenate([stale_v[1, :, :, :, cut].reshape(keys, HD), kv[h, 1].reshape(keys, HD)], axis=1)
        s_img = lax.dot_general(jnp.concatenate([q, q], axis=1), k_img, NT, preferred_element_type=F32)
        s_txt = lax.dot_general(q, text_v[0, :, cut], NT, preferred_element_type=F32)
        peak = jnp.maximum(jnp.max(s_img, axis=1, keepdims=True), jnp.max(s_txt, axis=1, keepdims=True))
        w_img = jnp.exp((s_img - peak) * scale).astype(BF)
        w_txt = jnp.exp((s_txt - peak) * scale).astype(BF)
        total = jnp.sum(w_img.astype(F32), axis=1, keepdims=True) + jnp.sum(w_txt.astype(F32), axis=1, keepdims=True)
        o_img = lax.dot_general(w_img, v_img, NN, preferred_element_type=F32)
        o_txt = lax.dot_general(w_txt, text_v[1, :, cut], NN, preferred_element_type=F32)
        o = (o_img[:, :HD] + o_img[:, HD:] + o_txt) / total
        stats = jnp.where(lane < 3, peak, total)
        third = lax.rem(lane, 3)
        top = stats.astype(BF).astype(F32)
        mid = (stats - top).astype(BF).astype(F32)
        low = stats - top - mid
        terms = jnp.where(third == 0, top, jnp.where(third == 1, mid, low))
        terms = terms.astype(BF)
        o_send[h, :, :rows] = o.astype(BF).reshape(QUAD, rows, HD)
        for v in range(QUAD):
            turned = lax.dot_general(first, terms[v * rows : (v + 1) * rows], NT, preferred_element_type=F32)
            o_send[h, v, rows:, :rows] = turned.astype(BF)
        for k in range(3):
            send(o_send.at[h, q_at[k]], o_recv.at[h, zq], o_s.at[h, k], o_r.at[h, zq], q_peers[k])

    pick_row = lax.broadcasted_iota(jnp.int32, (STATS, 2 * HD), 0)
    pick_col = lax.broadcasted_iota(jnp.int32, (STATS, 2 * HD), 1)
    pick = (lax.div(pick_row, 3) == lax.div(pick_col, HD)).astype(F32).astype(BF)

    def combine(h):
        o_recv[h, zq] = o_send[h, zq]
        for k in range(3):
            arrive(o_recv.at[h, q_at[k]], o_s.at[h, k], o_r.at[h, q_at[k]])
        wide = [
            lax.dot_general(o_recv[h, v, rows:, :rows], pick, TN, preferred_element_type=F32) for v in range(QUAD)
        ]
        peak = jnp.maximum(jnp.maximum(wide[0], wide[1]), jnp.maximum(wide[2], wide[3]))[:, :HD]
        shares = [jnp.exp((w[:, :HD] - peak) * scale) * w[:, HD:] for w in wide]
        mix = sum(shares[v] * o_recv[h, v, :rows].astype(F32) for v in range(QUAD)) / sum(shares)
        a_all[h, x] = mix.astype(BF)
        for k in range(3):
            send(a_all.at[h, x], a_all.at[h, x], a_s.at[h, k], a_r.at[h, x], x_peers[k])

    kv_half(0)
    kv_x()
    kv_half(1)
    kv_half(2)
    q_quad()
    kv_on(0)
    w_half()
    kv_core()
    kv_on(1)
    kv_on(2)
    kv_core_on(0)
    w_got_half()
    w_quad(far)
    kv_core_on(1)
    ready()
    kv_core_on(2)
    attend(0)
    attend(1)
    attend(2)
    combine(0)
    w_core(far)
    combine(1)
    w_quad(near)
    combine(2)

    for h in range(heads):
        for k in range(3):
            arrive(a_all.at[h, x_at[k]], a_s.at[h, k], a_r.at[h, x_at[k]])
    attended = jnp.concatenate([a_all[h].reshape(NX * rows, HD) for h in range(heads)], axis=1)

    def home(half):
        return pltpu.make_async_remote_copy(
            src_ref=p_send.at[half, x], dst_ref=p_recv.at[half, y], send_sem=p_s.at[half, 3], recv_sem=p_r.at[half, y],
            device_id=feature_home, device_id_type=MESH,
        )

    def project(half):
        side = near if half else far
        pieces = [wt[side, lax.rem(v + QUAD - zq, QUAD)].reshape(NC * rows, width) for v in range(QUAD)]
        term = lax.dot_general(attended, jnp.concatenate(pieces, axis=0), NT, preferred_element_type=F32)
        p_send[half] = term.astype(BF).reshape(NX, rows, width)

    def share(half):
        for k in range(3):
            send(p_send.at[half, x_at[k]], p_recv.at[half, y], p_s.at[half, k], p_r.at[half, y], feature_peers[k])

        @pl.when(away)
        def _():
            home(half).start()

        @pl.when(jnp.logical_not(away))
        def _():
            p_recv[half, y] = p_send[half, x]

    def gather(half):
        for k in range(3):
            arrive(p_recv.at[half, y_at[k]], p_s.at[half, k], p_r.at[half, y_at[k]])

        @pl.when(away)
        def _():
            home(half).wait_recv()

        return jnp.sum(p_recv[half].astype(F32), axis=0)

    w_done(far)
    project(0)
    share(0)
    w_core(near)
    w_done(near)
    project(1)
    z_send[...] = gather(0).astype(BF)
    pl.semaphore_wait(entered, 1)
    send(z_send, z_recv, zz_s, zz_r, zh_peer)
    share(1)
    rest = gather(1) + bias_v[...].reshape(1, width)
    arrive(z_recv, zz_s, zz_r)
    out_ref[...] = (gate_v[...].reshape(1, width) * (rest + z_recv[...].astype(F32))).astype(BF)
    for cp in pending:
        cp.wait_send()

    @pl.when(away)
    def _():
        for half in range(2):
            home(half).wait_send()


def body(queries, stale_kv, codes, exponents, text_kv, out_weight, out_bias, out_gate):
    rows, width = queries.shape
    heads = width // HD
    dma = pltpu.SemaphoreType.DMA
    any_spec = pl.BlockSpec(memory_space=pl.ANY)
    return pl.pallas_call(
        kernel,
        out_shape=jax.ShapeDtypeStruct((rows, width), BF),
        in_specs=[any_spec] * 8,
        out_specs=pl.BlockSpec(memory_space=pltpu.VMEM),
        scratch_shapes=[
            pltpu.VMEM(codes.shape, jnp.int32),
            pltpu.VMEM((heads, 2, rows), jnp.int32),
            pltpu.VMEM((width,), F32),
            pltpu.VMEM((width,), F32),
            pltpu.VMEM((2, NX, 2, NC * rows, width), BF),
            pltpu.VMEM((2, text_kv.shape[1] // QUAD, width), BF),
            pltpu.VMEM((QUAD, rows, width), BF),
            pltpu.VMEM((heads, 2, NX, 2, NC, rows, HD), BF),
            pltpu.VMEM((2, QUAD, NC, rows, width), BF),
            pltpu.VMEM((heads, QUAD, rows + STATS, HD), BF),
            pltpu.VMEM((heads, QUAD, rows + STATS, HD), BF),
            pltpu.VMEM((heads, NX, rows, HD), BF),
            pltpu.VMEM((2, NX, rows, width), BF),
            pltpu.VMEM((2, NY, rows, width), BF),
            pltpu.VMEM((rows, width), BF),
            pltpu.VMEM((rows, width), BF),
            dma((15,)),
            dma((3,)), dma((QUAD,)),
            dma((heads,)), dma((heads,)),
            dma((3,)), dma((NX,)),
            dma((heads, 3)), dma((heads, NX)),
            dma((heads + 1,)), dma((heads + 1,)),
            dma(()), dma(()),
            dma((2, 3)), dma((2, QUAD)),
            dma((2,)), dma((2,)),
            dma((heads, 3)), dma((heads, QUAD)),
            dma((heads, 3)), dma((heads, NX)),
            dma((2, 4)), dma((2, NY)),
            dma(()), dma(()),
            pltpu.SemaphoreType.REGULAR,
        ],
        compiler_params=pltpu.CompilerParams(
            collective_id=0, has_side_effects=True, vmem_limit_bytes=60 * 1024 * 1024
        ),
        cost_estimate=pl.CostEstimate(flops=640_000_000, bytes_accessed=4_000_000, transcendentals=520_000),
        name="joint_attention",
    )(
        queries, stale_kv, codes, exponents.transpose(2, 0, 1), text_kv, out_weight.T,
        out_bias, out_gate,
    )


def solution(mesh):
    placed = (
        P("patch", "head"),
        P(None, None, "head"),
        P(None, "patch", "head"),
        P(None, "patch", "head"),
        P(None, None, "head"),
        P("head", "patch"),
        P("head"),
        P("head"),
    )
    return jax.shard_map(
        body, mesh=mesh, in_specs=placed, out_specs=P("patch", "head"), check_vma=False
    )
```

time: 59.3 us -> 54.8 us (0.924)
  the two profiles are of different devices: /device:TPU:65 before, /device:TPU:6 now
where the time goes in v3:
time: 54.8 us; the launch traced here: 54.6 us
  Pallas kernels  53.2 us (97%)
  local copies, waits for them, and re-layouts  1.39 us (3%)
    pallas_call x1, Pallas kernels, body(): pl.pallas_call(kernel, out_shape=jax.ShapeDtypeStruct((rows, width), BF),...  53.2 us
    unnamed x1, local copies, waits for them, and re-layouts  1.39 us

profile of v3, /device:TPU:6, one launch (start us, length us, event | category | flops | bytes accessed | tf_op | source)
XLA Modules:
  0.0 54.6 jit_solution(4528346042919289288)
XLA Ops:
  0.0 53.2 %joint_attention.1 = bf16[48,384]{1,0:T(8,128)(2,1)} custom-call(bf16[48,384]{1,0:T(8,128)(2,1)} %q_hbm.1, bf16[2,3072,384]{2,1,0:T(8,128)(2,1)} %stale_hbm.1, s32[2,48,384]{2,1,0:T(8,128)} %codes_hbm.1, s32[3,2,48]{2,1,0:T(2,128)} %bitcast.3, bf16[2,512,384]{2,1,0:T(8,128)(2,1)} %text_hbm.1, bf16[48,384]{1,0:T(8,128)(2,1)} %bitcast.2, f32[384]{0:T(512)} %bias_hbm.1, ...), custom_call_target="tpu_custom_call" | custom-call | flops 640000000 | bytes 4000000 | tf_op jit(solution)/shard_map/joint_attention/pallas_call | solution.py:325
  53.2 1.4 %copy.10 = bf16[48,384]{1,0:T(8,128)(2,1)} copy(bf16[48,384]{1,0:T(8,128)(2,1)} %joint_attention.1) | data formatting | bytes 73728

commit v4 on v3

--- a/solution.py
+++ b/solution.py
@@ -299,11 +299,11 @@
     project(0)
     share(0)
     w_core(near)
-    w_done(near)
-    project(1)
     z_send[...] = gather(0).astype(BF)
     pl.semaphore_wait(entered, 1)
     send(z_send, z_recv, zz_s, zz_r, zh_peer)
+    w_done(near)
+    project(1)
     share(1)
     rest = gather(1) + bias_v[...].reshape(1, width)
     arrive(z_recv, zz_s, zz_r)
@@ -324,7 +324,7 @@
     any_spec = pl.BlockSpec(memory_space=pl.ANY)
     return pl.pallas_call(
         kernel,
-        out_shape=jax.ShapeDtypeStruct((rows, width), BF),
+        out_shape=pltpu.VMEM((rows, width), BF),
         in_specs=[any_spec] * 8,
         out_specs=pl.BlockSpec(memory_space=pltpu.VMEM),
         scratch_shapes=[

time: 54.8 us -> 53.4 us (0.974)
  local copies, waits for them, and re-layouts: 1.39 us -> 0.62 us
  Pallas kernels: 53.2 us -> 52.6 us
    unnamed x1, local copies, waits for them, and re-layouts: 1.39 us -> 0.62 us
    pallas_call x1, Pallas kernels: 53.2 us -> 52.6 us  [body(): pl.pallas_call(kernel, out_shape=pltpu.VMEM((rows, width), BF), in_specs=...]
where the time goes in v4:
time: 53.4 us; the launch traced here: 53.2 us
  Pallas kernels  52.6 us (99%)
  local copies, waits for them, and re-layouts  0.62 us (1%)
    pallas_call x1, Pallas kernels, body(): pl.pallas_call(kernel, out_shape=pltpu.VMEM((rows, width), BF), in_specs=...  52.6 us

profile of v4, /device:TPU:6, one launch (start us, length us, event | category | flops | bytes accessed | tf_op | source)
XLA Modules:
  0.0 53.2 jit_solution(14359341210248132340)
XLA Ops:
  0.0 52.6 %joint_attention.1 = bf16[48,384]{1,0:T(8,128)(2,1)S(1)} custom-call(bf16[48,384]{1,0:T(8,128)(2,1)} %q_hbm.1, bf16[2,3072,384]{2,1,0:T(8,128)(2,1)} %stale_hbm.1, s32[2,48,384]{2,1,0:T(8,128)} %codes_hbm.1, s32[3,2,48]{2,1,0:T(2,128)} %bitcast.3, bf16[2,512,384]{2,1,0:T(8,128)(2,1)} %text_hbm.1, bf16[48,384]{1,0:T(8,128)(2,1)} %bitcast.2, f32[384]{0:T(512)} %bias_hbm.1, ...), custom_call_target="tpu_custom_call" | custom-call | flops 640000000 | bytes 4000000 | tf_op jit(solution)/shard_map/joint_attention/pallas_call | solution.py:325
  52.6 0.6 %copy.10 = bf16[48,384]{1,0:T(8,128)(2,1)} copy(bf16[48,384]{1,0:T(8,128)(2,1)S(1)} %joint_attention.1) | data formatting | bytes 73728

commit v5 on v4

--- a/solution.py
+++ b/solution.py
@@ -236,9 +236,9 @@
     kv_half(1)
     kv_half(2)
     q_quad()
+    kv_core()
     kv_on(0)
     w_half()
-    kv_core()
     kv_on(1)
     kv_on(2)
     kv_core_on(0)
@@ -261,60 +261,72 @@
             arrive(a_all.at[h, x_at[k]], a_s.at[h, k], a_r.at[h, x_at[k]])
     attended = jnp.concatenate([a_all[h].reshape(NX * rows, HD) for h in range(heads)], axis=1)
 
-    def home(half):
+    def columns(t):
+        return (1, pl.ds(0, width)) if t == heads else (0, pl.ds(t * HD, HD))
+
+    def home(t):
+        half, span = columns(t)
         return pltpu.make_async_remote_copy(
-            src_ref=p_send.at[half, x], dst_ref=p_recv.at[half, y], send_sem=p_s.at[half, 3], recv_sem=p_r.at[half, y],
-            device_id=feature_home, device_id_type=MESH,
+            src_ref=p_send.at[half, x, :, span], dst_ref=p_recv.at[half, y, :, span],
+            send_sem=p_s.at[t, 3], recv_sem=p_r.at[t, y], device_id=feature_home, device_id_type=MESH,
         )
 
-    def project(half):
-        side = near if half else far
-        pieces = [wt[side, lax.rem(v + QUAD - zq, QUAD)].reshape(NC * rows, width) for v in range(QUAD)]
-        term = lax.dot_general(attended, jnp.concatenate(pieces, axis=0), NT, preferred_element_type=F32)
-        p_send[half] = term.astype(BF).reshape(NX, rows, width)
-
-    def share(half):
-        for k in range(3):
-            send(p_send.at[half, x_at[k]], p_recv.at[half, y], p_s.at[half, k], p_r.at[half, y], feature_peers[k])
+    def project(t):
+        half, span = columns(t)
+        for k in (1, 0, 2):
+            send(p_send.at[half, x_at[k], :, span], p_recv.at[half, y, :, span], p_s.at[t, k], p_r.at[t, y], feature_peers[k])
 
         @pl.when(away)
         def _():
-            home(half).start()
+            home(t).start()
 
         @pl.when(jnp.logical_not(away))
         def _():
-            p_recv[half, y] = p_send[half, x]
-
-    def gather(half):
-        for k in range(3):
-            arrive(p_recv.at[half, y_at[k]], p_s.at[half, k], p_r.at[half, y_at[k]])
+            p_recv[half, y, :, span] = p_send[half, x, :, span]
+
+    def product(side, rows_of):
+        pieces = [wt[side, lax.rem(v + QUAD - zq, QUAD)].reshape(NC * rows, width) for v in range(QUAD)]
+        block = jnp.concatenate(pieces, axis=0)[rows_of]
+        term = lax.dot_general(attended, block, NT, preferred_element_type=F32).astype(BF)
+        return term.reshape(NX, rows, term.shape[1])
+
+    def gather(t):
+        half, span = columns(t)
+        for k in range(3):
+            arrive(p_recv.at[half, y_at[k], :, span], p_s.at[t, k], p_r.at[t, y_at[k]])
 
         @pl.when(away)
         def _():
-            home(half).wait_recv()
-
-        return jnp.sum(p_recv[half].astype(F32), axis=0)
+            home(t).wait_recv()
+
+        return jnp.sum(p_recv[half, :, :, span].astype(F32), axis=0)
 
     w_done(far)
-    project(0)
-    share(0)
+    for t in range(heads):
+        p_send[0, :, :, t * HD : (t + 1) * HD] = product(far, slice(t * HD, (t + 1) * HD))
+        project(t)
     w_core(near)
-    z_send[...] = gather(0).astype(BF)
-    pl.semaphore_wait(entered, 1)
-    send(z_send, z_recv, zz_s, zz_r, zh_peer)
+    for t in range(heads):
+        span = pl.ds(t * HD, HD)
+        z_send[:, span] = gather(t).astype(BF)
+        if t == 0:
+            pl.semaphore_wait(entered, 1)
+        send(z_send.at[:, span], z_recv.at[:, span], zz_s.at[t], zz_r.at[t], zh_peer)
     w_done(near)
-    project(1)
-    share(1)
-    rest = gather(1) + bias_v[...].reshape(1, width)
-    arrive(z_recv, zz_s, zz_r)
+    p_send[1] = product(near, slice(0, width))
+    project(heads)
+    rest = gather(heads) + bias_v[...].reshape(1, width)
+    for t in range(heads):
+        span = pl.ds(t * HD, HD)
+        arrive(z_recv.at[:, span], zz_s.at[t], zz_r.at[t])
     out_ref[...] = (gate_v[...].reshape(1, width) * (rest + z_recv[...].astype(F32))).astype(BF)
     for cp in pending:
         cp.wait_send()
 
     @pl.when(away)
     def _():
-        for half in range(2):
-            home(half).wait_send()
+        for t in range(heads + 1):
+            home(t).wait_send()
 
 
 def body(queries, stale_kv, codes, exponents, text_kv, out_weight, out_bias, out_gate):
@@ -355,8 +367,8 @@
             dma((2,)), dma((2,)),
             dma((heads, 3)), dma((heads, QUAD)),
             dma((heads, 3)), dma((heads, NX)),
-            dma((2, 4)), dma((2, NY)),
-            dma(()), dma(()),
+            dma((heads + 1, 4)), dma((heads + 1, NY)),
+            dma((heads,)), dma((heads,)),
             pltpu.SemaphoreType.REGULAR,
         ],
         compiler_params=pltpu.CompilerParams(

time: 53.4 us -> 52.7 us (0.987)
  Pallas kernels: 52.6 us -> 51.8 us
    pallas_call x1, Pallas kernels: 52.6 us -> 51.8 us  [body(): pl.pallas_call(kernel, out_shape=pltpu.VMEM((rows, width), BF), in_specs=...]
where the time goes in v5:
time: 52.7 us; the launch traced here: 52.4 us
  Pallas kernels  51.8 us (98%)
  local copies, waits for them, and re-layouts  0.62 us (1%)
    pallas_call x1, Pallas kernels, body(): pl.pallas_call(kernel, out_shape=pltpu.VMEM((rows, width), BF), in_specs=...  51.8 us

profile of v5, /device:TPU:6, one launch (start us, length us, event | category | flops | bytes accessed | tf_op | source)
XLA Modules:
  0.0 52.4 jit_solution(16349649352840898339)
XLA Ops:
  0.0 51.8 %joint_attention.1 = bf16[48,384]{1,0:T(8,128)(2,1)S(1)} custom-call(bf16[48,384]{1,0:T(8,128)(2,1)} %q_hbm.1, bf16[2,3072,384]{2,1,0:T(8,128)(2,1)} %stale_hbm.1, s32[2,48,384]{2,1,0:T(8,128)} %codes_hbm.1, s32[3,2,48]{2,1,0:T(2,128)} %bitcast.3, bf16[2,512,384]{2,1,0:T(8,128)(2,1)} %text_hbm.1, bf16[48,384]{1,0:T(8,128)(2,1)} %bitcast.2, f32[384]{0:T(512)} %bias_hbm.1, ...), custom_call_target="tpu_custom_call" | custom-call | flops 640000000 | bytes 4000000 | tf_op jit(solution)/shard_map/joint_attention/pallas_call | solution.py:337
  51.8 0.6 %copy.10 = bf16[48,384]{1,0:T(8,128)(2,1)} copy(bf16[48,384]{1,0:T(8,128)(2,1)S(1)} %joint_attention.1) | data formatting | bytes 73728

commit v6 on v5

--- a/solution.py
+++ b/solution.py
@@ -118,7 +118,7 @@
         send(mine, mine, kh_s.at[h], kh_r.at[h], half_peer)
 
     def kv_x():
-        for k in range(3):
+        for k in (1, 0, 2):
             mine = kv.at[:, :, x, zb, c]
             send(mine, mine, kx_s.at[k], kx_r.at[x], x_peers[k])
 
@@ -151,7 +151,7 @@
     def kv_on(h):
         slot = kv.at[h, :, x, 1 - zb, c]
         arrive(slot, kh_s.at[h], kh_r.at[h])
-        for k in range(3):
+        for k in (1, 0, 2):
             send(slot, slot, kf_s.at[h, k], kf_r.at[h, x], x_peers[k])
 
     def kv_core():
@@ -228,7 +228,7 @@
         shares = [jnp.exp((w[:, :HD] - peak) * scale) * w[:, HD:] for w in wide]
         mix = sum(shares[v] * o_recv[h, v, :rows].astype(F32) for v in range(QUAD)) / sum(shares)
         a_all[h, x] = mix.astype(BF)
-        for k in range(3):
+        for k in (1, 0, 2):
             send(a_all.at[h, x], a_all.at[h, x], a_s.at[h, k], a_r.at[h, x], x_peers[k])
 
     kv_half(0)

time: 52.7 us -> 52.6 us (level)
  no operation moved by 1% of the time
where the time goes in v6:
time: 52.6 us; the launch traced here: 52.4 us
  Pallas kernels  51.7 us (98%)
  local copies, waits for them, and re-layouts  0.62 us (1%)
    pallas_call x1, Pallas kernels, body(): pl.pallas_call(kernel, out_shape=pltpu.VMEM((rows, width), BF), in_specs=...  51.7 us

profile of v6, /device:TPU:6, one launch (start us, length us, event | category | flops | bytes accessed | tf_op | source)
XLA Modules:
  0.0 52.4 jit_solution(10572850141310037035)
XLA Ops:
  0.0 51.7 %joint_attention.1 = bf16[48,384]{1,0:T(8,128)(2,1)S(1)} custom-call(bf16[48,384]{1,0:T(8,128)(2,1)} %q_hbm.1, bf16[2,3072,384]{2,1,0:T(8,128)(2,1)} %stale_hbm.1, s32[2,48,384]{2,1,0:T(8,128)} %codes_hbm.1, s32[3,2,48]{2,1,0:T(2,128)} %bitcast.3, bf16[2,512,384]{2,1,0:T(8,128)(2,1)} %text_hbm.1, bf16[48,384]{1,0:T(8,128)(2,1)} %bitcast.2, f32[384]{0:T(512)} %bias_hbm.1, ...), custom_call_target="tpu_custom_call" | custom-call | flops 640000000 | bytes 4000000 | tf_op jit(solution)/shard_map/joint_attention/pallas_call | solution.py:337
  51.7 0.6 %copy.10 = bf16[48,384]{1,0:T(8,128)(2,1)} copy(bf16[48,384]{1,0:T(8,128)(2,1)S(1)} %joint_attention.1) | data formatting | bytes 73728

commit v7 on v6

--- a/solution.py
+++ b/solution.py
@@ -246,8 +246,8 @@
     w_quad(far)
     kv_core_on(1)
     ready()
+    attend(0)
     kv_core_on(2)
-    attend(0)
     attend(1)
     attend(2)
     combine(0)

time: 52.6 us -> 52.6 us (level)
  no operation moved by 1% of the time
where the time goes in v7:
time: 52.6 us; the launch traced here: 52.4 us
  Pallas kernels  51.7 us (98%)
  local copies, waits for them, and re-layouts  0.62 us (1%)
    pallas_call x1, Pallas kernels, body(): pl.pallas_call(kernel, out_shape=pltpu.VMEM((rows, width), BF), in_specs=...  51.7 us

profile of v7, /device:TPU:6, one launch (start us, length us, event | category | flops | bytes accessed | tf_op | source)
XLA Modules:
  0.0 52.4 jit_solution(16721665595112761768)
XLA Ops:
  0.0 51.7 %joint_attention.1 = bf16[48,384]{1,0:T(8,128)(2,1)S(1)} custom-call(bf16[48,384]{1,0:T(8,128)(2,1)} %q_hbm.1, bf16[2,3072,384]{2,1,0:T(8,128)(2,1)} %stale_hbm.1, s32[2,48,384]{2,1,0:T(8,128)} %codes_hbm.1, s32[3,2,48]{2,1,0:T(2,128)} %bitcast.3, bf16[2,512,384]{2,1,0:T(8,128)(2,1)} %text_hbm.1, bf16[48,384]{1,0:T(8,128)(2,1)} %bitcast.2, f32[384]{0:T(512)} %bias_hbm.1, ...), custom_call_target="tpu_custom_call" | custom-call | flops 640000000 | bytes 4000000 | tf_op jit(solution)/shard_map/joint_attention/pallas_call | solution.py:337
  51.7 0.6 %copy.10 = bf16[48,384]{1,0:T(8,128)(2,1)} copy(bf16[48,384]{1,0:T(8,128)(2,1)S(1)} %joint_attention.1) | data formatting | bytes 73728
